TPU v7x, 512 devices: a whole 4x4x16 slice. The times are simulated.
512 devices in a mesh: group: 16 (over z_lo, core), blk: 32 (over x, y, z_hi).
Axes of the slice: x: 4, y: 4, z: 16 (z_hi: 2, z_lo: 8; z = z_hi * 8 + z_lo), core: 2. Of those that a mesh axis runs over, the one named last changes fastest.
Arguments:
- image_emb: bfloat16 [262144, 1152], P(('group', 'blk')), may hold values from -0.1875 to 0.1875
- text_emb: bfloat16 [262144, 1152], P(('group', 'blk')), may hold values from -0.1875 to 0.1875
- labels: int32 [262144], P(('group', 'blk')), may hold values from 0 to 511, as said below
- log_scale: float32 [1], replicated, may hold values from 1 to 2
- bias: float32 [1], replicated, may hold values from -1.5 to -0.5
Outputs:
- grad_image: bfloat16 [262144, 1152], P(('group', 'blk'))
- grad_text: bfloat16 [262144, 1152], P(('group', 'blk'))
Inputs may be any that keep to these rules, and one draw needn't show every extreme that they name: `labels`: within each aligned block of 512 rows the entries are a permutation of 0 to 511.
All inputs are finite; a program needn't handle non-finite values.
Results may differ from a plain program's by a relative error of at most 0.0064.
Values may be sent and summed in bfloat16 or wider, within the bound.
A program may use at most 64 MiB of HBM per device.

v0:
```python
import jax
import jax.numpy as jnp
from jax import lax
from jax.sharding import PartitionSpec as P

EPS = 1e-06


def passed_along(value, axis, steps):
    count = lax.axis_size(axis)
    pairs = [(source, (source + steps) % count) for source in range(count)]
    return lax.ppermute(value, axis, pairs)


def unit_rows(v):
    f = v.astype(jnp.float32)
    inv = lax.rsqrt(jnp.sum(f * f, axis=-1, keepdims=True) + EPS)
    return (f * inv, inv)


def tile_terms(xh, yh, scale, shift_b, label):
    s = (
        scale
        * lax.dot_general(xh, yh, (((1,), (1,)), ((), ())), preferred_element_type=jnp.float32)
        + shift_b
    )
    q = (jax.nn.sigmoid(s) - label).astype(jnp.bfloat16)
    dx = scale * jnp.dot(q, yh, preferred_element_type=jnp.float32)
    dy = scale * lax.dot_general(
        q, xh, (((0,), (0,)), ((), ())), preferred_element_type=jnp.float32
    )
    return (dx, dy)


def shards(image_emb, text_emb, labels, log_scale, bias):
    scale = jnp.exp(log_scale[0])
    shift_b = bias[0]
    ximg, xinv = unit_rows(image_emb)
    ytxt, yinv = unit_rows(text_emb)
    xh = ximg.astype(jnp.bfloat16)
    yh = ytxt.astype(jnp.bfloat16)
    columns = jnp.arange(labels.shape[0], dtype=jnp.int32)
    onehot = (labels[:, None] == columns[None, :]).astype(jnp.float32)
    text_cycle = passed_along(text_emb, "blk", 1)
    text_group = passed_along(text_emb, "group", 1)
    cycle_unit, _ = unit_rows(text_cycle)
    group_unit, _ = unit_rows(text_group)
    dx_own, dy_own = tile_terms(xh, yh, scale, shift_b, onehot)
    dx_cycle, dy_cycle = tile_terms(xh, cycle_unit.astype(jnp.bfloat16), scale, shift_b, 0.0)
    dx_group, dy_group = tile_terms(xh, group_unit.astype(jnp.bfloat16), scale, shift_b, 0.0)
    dxh = dx_own + dx_cycle + dx_group
    back_cycle = passed_along(dy_cycle.astype(jnp.bfloat16), "blk", -1)
    back_group = passed_along(dy_group.astype(jnp.bfloat16), "group", -1)
    dyh = dy_own + back_cycle.astype(jnp.float32) + back_group.astype(jnp.float32)
    grad_image = ((dxh - ximg * jnp.sum(ximg * dxh, axis=-1, keepdims=True)) * xinv).astype(
        jnp.bfloat16
    )
    grad_text = ((dyh - ytxt * jnp.sum(ytxt * dyh, axis=-1, keepdims=True)) * yinv).astype(
        jnp.bfloat16
    )
    return (grad_image, grad_text)


def solution(mesh):
    placed = (P(("group", "blk"), None), P(("group", "blk"), None), P(("group", "blk")), P(), P())
    return jax.shard_map(
        shards,
        mesh=mesh,
        in_specs=placed,
        out_specs=(P(("group", "blk"), None), P(("group", "blk"), None)),
        check_vma=False,
    )
```

profile of v0, /device:TPU:40, one launch (start us, length us, event | category | flops | bytes accessed | tf_op | source)
XLA Modules:
  0.0 264.0 jit_solution(17532291264414861476)
XLA Ops:
  0.6 0.0 copy-start
  0.6 0.0 copy-start.1
  0.7 0.0 copy-start.2
  0.7 15.0 %collective-permute-start = (bf16[512,1152]{1,0:T(8,128)(2,1)}, bf16[512,1152]{1,0:T(8,128)(2,1)S(1)}, u32[]{:S(2)}, u32[]{:S(2)}) collective-permute-start(bf16[512,1152]{1,0:T(8,128)(2,1)} %param.6), channel_id=1, source_target_pairs={{0,1},{1,2},{2,3},{3,4},{4,5},{5,6},{6,7},{7,8},{8,9},{9,10},{10,1... | collective-permute-start | bytes 3538952 | tf_op jit(solution)/shard_map/ppermute | solution.py:12
  15.6 1.9 collective-permute-start.1
  17.6 1.6 fusion.18
  19.1 1.6 fusion.13
  22.1 0.0 copy-done
  22.1 0.0 copy-done.1
  22.1 0.0 copy-done.2
  22.1 1.2 fusion.39
  23.3 1.0 fusion.46
  24.3 105.5 %collective-permute-done = bf16[512,1152]{1,0:T(8,128)(2,1)S(1)} collective-permute-done((bf16[512,1152]{1,0:T(8,128)(2,1)}, bf16[512,1152]{1,0:T(8,128)(2,1)S(1)}, u32[]{:S(2)}, u32[]{:S(2)}) %collective-permute-start) | collective-permute-done | bytes 1179680 | tf_op jit(solution)/shard_map/ppermute | solution.py:12
  129.8 0.3 fusion.19
  130.1 0.1 collective-permute-done.1
  130.3 0.3 fusion.21
  130.6 1.1 fusion.40
  131.7 1.0 fusion.2
  132.7 1.9 collective-permute-start.3
  134.6 1.1 fusion.41
  135.8 0.9 fusion.1
  136.7 12.9 %collective-permute-start.2 = (bf16[512,1152]{1,0:T(8,128)(2,1)S(1)}, bf16[512,1152]{1,0:T(8,128)(2,1)S(1)}, u32[]{:S(2)}, u32[]{:S(2)}) collective-permute-start(bf16[512,1152]{1,0:T(8,128)(2,1)S(1)} %fusion.1), channel_id=1, source_target_pairs={{0,31},{1,0},{2,1},{3,2},{4,3},{5,4},{6,5},{7,6},{8,7},{9,8},{10,9... | collective-permute-start | bytes 3538952 | tf_op jit(solution)/shard_map/ppermute | solution.py:12
  149.6 1.0 convolution_add_fusion.1
  150.6 1.3 fusion.9
  151.9 1.5 fusion.12
  153.4 23.2 %collective-permute-done.3 = bf16[512,1152]{1,0:T(8,128)(2,1)S(1)} collective-permute-done((bf16[512,1152]{1,0:T(8,128)(2,1)S(1)}, bf16[512,1152]{1,0:T(8,128)(2,1)S(1)}, u32[]{:S(2)}, u32[]{:S(2)}) %collective-permute-start.3) | collective-permute-done | bytes 1179680 | tf_op jit(solution)/shard_map/ppermute | solution.py:12
  176.6 84.4 %collective-permute-done.2 = bf16[512,1152]{1,0:T(8,128)(2,1)S(1)} collective-permute-done((bf16[512,1152]{1,0:T(8,128)(2,1)S(1)}, bf16[512,1152]{1,0:T(8,128)(2,1)S(1)}, u32[]{:S(2)}, u32[]{:S(2)}) %collective-permute-start.2) | collective-permute-done | bytes 1179680 | tf_op jit(solution)/shard_map/ppermute | solution.py:12
  261.0 1.5 fusion.14
  262.5 1.5 fusion.17
  (4 shorter events, 0.0 us)
Async XLA Ops:
  0.6 21.4 %copy-start = (bf16[512,1152]{1,0:T(8,128)(2,1)S(1)}, bf16[512,1152]{1,0:T(8,128)(2,1)}, u32[]{:S(2)}) copy-start(bf16[512,1152]{1,0:T(8,128)(2,1)} %param.6) | copy-start | bytes 3538948
  0.6 21.4 %copy-start.1 = (bf16[512,1152]{1,0:T(8,128)(2,1)S(1)}, bf16[512,1152]{1,0:T(8,128)(2,1)}, u32[]{:S(2)}) copy-start(bf16[512,1152]{1,0:T(8,128)(2,1)} %param.5) | copy-start | bytes 3538948
  0.7 21.4 %copy-start.2 = (s32[512]{0:T(512)S(1)}, s32[512]{0:T(512)}, u32[]{:S(2)}) copy-start(s32[512]{0:T(512)} %param.7) | copy-start | bytes 6148
  0.7 129.2 %collective-permute-start = (bf16[512,1152]{1,0:T(8,128)(2,1)}, bf16[512,1152]{1,0:T(8,128)(2,1)S(1)}, u32[]{:S(2)}, u32[]{:S(2)}) collective-permute-start(bf16[512,1152]{1,0:T(8,128)(2,1)} %param.6), channel_id=1, source_target_pairs={{0,1},{1,2},{2,3},{3,4},{4,5},{5,6},{6,7},{7,8},{8,9},{9,10},{10,1... | collective-permute-start | bytes 3538952 | tf_op jit(solution)/shard_map/ppermute | solution.py:12
  15.6 114.6 %collective-permute-start.1 = (bf16[512,1152]{1,0:T(8,128)(2,1)}, bf16[512,1152]{1,0:T(8,128)(2,1)S(1)}, u32[]{:S(2)}, u32[]{:S(2)}) collective-permute-start(bf16[512,1152]{1,0:T(8,128)(2,1)} %param.6), channel_id=1, source_target_pairs={{0,32},{32,64},{64,96},{96,128},{128,160},{160,192},{192,224},{224... | collective-permute-start | bytes 3538952 | tf_op jit(solution)/shard_map/ppermute | solution.py:12
  132.7 43.9 %collective-permute-start.3 = (bf16[512,1152]{1,0:T(8,128)(2,1)S(1)}, bf16[512,1152]{1,0:T(8,128)(2,1)S(1)}, u32[]{:S(2)}, u32[]{:S(2)}) collective-permute-start(bf16[512,1152]{1,0:T(8,128)(2,1)S(1)} %fusion.2), channel_id=1, source_target_pairs={{0,480},{32,0},{64,32},{96,64},{128,96},{160,128},{192,160},{224,1... | collective-permute-start | bytes 3538952 | tf_op jit(solution)/shard_map/ppermute | solution.py:12
  136.7 124.3 %collective-permute-start.2 = (bf16[512,1152]{1,0:T(8,128)(2,1)S(1)}, bf16[512,1152]{1,0:T(8,128)(2,1)S(1)}, u32[]{:S(2)}, u32[]{:S(2)}) collective-permute-start(bf16[512,1152]{1,0:T(8,128)(2,1)S(1)} %fusion.1), channel_id=1, source_target_pairs={{0,31},{1,0},{2,1},{3,2},{4,3},{5,4},{6,5},{7,6},{8,7},{9,8},{10,9... | collective-permute-start | bytes 3538952 | tf_op jit(solution)/shard_map/ppermute | solution.py:12
where the time goes:
time: 264 us
  waiting for transfers between devices  213 us (81%)
  starting transfers between devices  31.7 us (12%)
  matrix products  10.2 us (4%)
  other arithmetic  6.82 us (3%)
    ppermute x4, waiting for transfers between devices, passed_along(): return lax.ppermute(value, axis, pairs)  213 us
    ppermute x4, starting transfers between devices, passed_along(): return lax.ppermute(value, axis, pairs)  31.7 us
  transfers between devices with their start and end apart: 4, of which 4 were waited for; matrix products, arithmetic and copies ran while one was open for 4% of the time, Pallas kernels for 0%

commit v1 on v0

v1 whole, which is shorter than its diff:
```python
import functools

import jax
import jax.numpy as jnp
from jax import lax
from jax.experimental import pallas as pl
from jax.experimental.pallas import tpu as pltpu
from jax.sharding import PartitionSpec as P

EPS = 1e-06
MESH = pl.DeviceIdType.MESH
TEXT, IMAGE = 0, 1
HOPS = 8
WAVES = 2
CHUNKS = 4
GROUP_SLOT, LAST_SLOT = 7, 8
BAND = 128


def dot_nt(a, b):
    return lax.dot_general(a, b, (((1,), (1,)), ((), ())), preferred_element_type=jnp.float32)


def dot_tn(a, b):
    return lax.dot_general(a, b, (((0,), (0,)), ((), ())), preferred_element_type=jnp.float32)


def unit_rows(v):
    f = v.astype(jnp.float32)
    inv = lax.rsqrt(jnp.sum(f * f, axis=-1, keepdims=True) + EPS)
    return f * inv, inv


def kernel(
    rows, compute, scale_ref, bias_ref, label_ref, image_ref, text_ref, gimage_ref, gtext_ref,
    raw, unit, acc, piece_unit, stage, buf, load_sem, send_sem, recv_sem, side_sem, store_sem,
):
    g, b = lax.axis_index("group"), lax.axis_index("blk")
    core, z_lo = lax.rem(g, 2), lax.div(g, 2)
    z_hi, xy = lax.rem(b, 2), lax.div(b, 2)
    z = z_hi * 8 + z_lo
    other = 1 - core

    def device(z_to, core_to, xy_to):
        z_in = lax.rem(z_to + 32, 16)
        return lax.rem(z_in, 8) * 2 + core_to, lax.rem(xy_to + 16, 16) * 2 + lax.div(z_in, 8)

    def way(c):
        return 2 * c - 1

    def lane_core(lane, z_at, c):
        edge = 7 if lane == TEXT else 0
        return jnp.where(lax.rem(z_at + 32, 8) == edge, 1 - c, c)

    step = way(core)
    following, before = device(z + step, core, xy), device(z - step, core, xy)
    partner = device(z, other, xy)
    first, first_from, last, last_from = [], [], [], []
    for lane in (TEXT, IMAGE):
        own_lane = lane_core(lane, z, core)
        first.append(device(z + way(own_lane), own_lane, xy))
        first_from.append(device(z - step, lane_core(lane, z - step, core), xy))
        crossing = 0 if lane == TEXT else 1
        shift = 1 if lane == TEXT else -1
        last_hi = lax.div(lax.rem(z + step + 32, 16), 8)
        last.append(
            device(z + step, lane_core(lane, z + step, core), xy + jnp.where(last_hi == crossing, shift, 0))
        )
        last_from.append(
            device(z - way(own_lane), own_lane, xy - jnp.where(z_hi == crossing, shift, 0))
        )

    own = (text_ref, image_ref)
    part = rows // (WAVES * CHUNKS)
    wave_rows = rows // WAVES

    loads = [pltpu.make_async_copy(own[l], raw.at[l], load_sem.at[l]) for l in (TEXT, IMAGE)]
    for load in loads:
        load.start()

    barrier = pltpu.get_barrier_semaphore()
    for source in (before, partner, *first_from, *last_from):
        pl.semaphore_signal(barrier, inc=1, device_id=source, device_id_type=MESH)
    pl.semaphore_wait(barrier, 6)

    def chunk_rows(chunk):
        return pl.ds(pl.multiple_of(chunk * part, part), part)

    def hop(lane, src, slot, hop_at, chunk, to):
        at = chunk_rows(chunk)
        return pltpu.make_async_remote_copy(
            src_ref=src.at[at], dst_ref=buf.at[lane, slot, at], send_sem=send_sem.at[lane, hop_at],
            recv_sem=recv_sem.at[lane, slot, chunk], device_id=to, device_id_type=MESH,
        )

    def arrived(lane, slot, chunk):
        hop(lane, buf.at[lane, slot], slot, 0, chunk, following).wait_recv()

    own_side = core
    lane_side = other
    gives = jnp.where(core == 0, z_lo != 7, z_lo != 0)
    takes_lane = jnp.where(core == 0, z_lo == 0, z_lo == 7)

    def side(src, lane, kind, chunk):
        at = chunk_rows(chunk)
        return pltpu.make_async_remote_copy(
            src_ref=src.at[at], dst_ref=buf.at[lane, GROUP_SLOT, at], send_sem=side_sem.at[kind],
            recv_sem=recv_sem.at[lane, GROUP_SLOT, chunk], device_id=partner, device_id_type=MESH,
        )

    def first_round(w):
        for lane in (TEXT, IMAGE):
            @pl.loop(0, CHUNKS)
            def _(c):
                hop(lane, own[lane], 0, 0, w * CHUNKS + c, first[lane]).start()

        for lane in (TEXT, IMAGE):
            @pl.when(own_side == lane)
            def _():
                @pl.loop(0, CHUNKS)
                def _(c):
                    side(own[lane], lane, 0, w * CHUNKS + c).start()

    def relay_round(w, h):
        for lane in (TEXT, IMAGE):
            @pl.loop(0, CHUNKS)
            def _(c):
                chunk = w * CHUNKS + c
                arrived(lane, h - 1, chunk)
                hop(lane, buf.at[lane, h - 1], h, h, chunk, following).start()

                @pl.when((h == 1) & gives & (lane_side == lane))
                def _():
                    side(buf.at[lane, 0], lane, 1, chunk).start()

    def last_round(w):
        for lane in (TEXT, IMAGE):
            @pl.loop(0, CHUNKS)
            def _(c):
                chunk = w * CHUNKS + c
                arrived(lane, HOPS - 2, chunk)
                hop(lane, buf.at[lane, HOPS - 2], LAST_SLOT, HOPS - 1, chunk, last[lane]).start()

    scale = jnp.exp(jnp.full((1, 1), scale_ref[0], jnp.float32))
    shift_b = bias_ref[0]

    def prepare():
        for l in (TEXT, IMAGE):
            loads[l].wait()

            @pl.loop(0, rows // BAND)
            def _(i):
                at = pl.ds(pl.multiple_of(i * BAND, BAND), BAND)
                unit[l, at] = unit_rows(raw[l, at])[0].astype(jnp.bfloat16)

    def own_tile():
        acc[TEXT] = jnp.zeros_like(acc[TEXT])

        @pl.loop(0, rows // BAND)
        def _(i):
            at = pl.ds(pl.multiple_of(i * BAND, BAND), BAND)
            s = scale * dot_nt(unit[TEXT, at], unit[IMAGE]) + shift_b
            text_row = lax.broadcasted_iota(jnp.int32, s.shape, 0) + i * BAND
            label = (text_row == label_ref[...]).astype(jnp.float32)
            q = (jax.nn.sigmoid(s) - label).astype(jnp.bfloat16)
            acc[IMAGE, at] = jnp.dot(q, unit[IMAGE], preferred_element_type=jnp.float32)
            acc[TEXT] += dot_tn(q, unit[TEXT, at])

    def piece(lane, slot, start, count):
        piece_unit[0:count] = unit_rows(buf[lane, slot, pl.ds(start, count)])[0].astype(jnp.bfloat16)

        @pl.loop(0, rows // BAND)
        def _(i):
            at = pl.ds(pl.multiple_of(i * BAND, BAND), BAND)
            s = scale * dot_nt(unit[1 - lane, at], piece_unit[0:count]) + shift_b
            q = jax.nn.sigmoid(s).astype(jnp.bfloat16)
            acc[lane, at] += jnp.dot(q, piece_unit[0:count], preferred_element_type=jnp.float32)

    def group_pieces(w):
        slot = jnp.where(takes_lane, HOPS - 2, GROUP_SLOT)
        for lane in (TEXT, IMAGE):
            from_lane = takes_lane & (core == lane)

            @pl.when(jnp.logical_not(from_lane))
            def _():
                @pl.loop(0, CHUNKS)
                def _(c):
                    arrived(lane, GROUP_SLOT, w * CHUNKS + c)

            if compute:
                piece(lane, jnp.where(from_lane, HOPS - 2, GROUP_SLOT), w * wave_rows, wave_rows)

    def last_pieces(w):
        for lane in (TEXT, IMAGE):
            @pl.loop(0, CHUNKS)
            def _(c):
                arrived(lane, LAST_SLOT, w * CHUNKS + c)

            if compute:
                piece(lane, LAST_SLOT, w * wave_rows, wave_rows)

    def store(lane):
        out = (gimage_ref, gtext_ref)[lane]
        return pltpu.make_async_copy(stage.at[lane], out, store_sem.at[lane])

    def finish(lane):
        @pl.loop(0, rows // BAND)
        def _(i):
            at = pl.ds(pl.multiple_of(i * BAND, BAND), BAND)
            u, inv = unit_rows(raw[1 - lane, at])
            d = scale * acc[lane, at]
            d = (d - u * jnp.sum(u * d, axis=-1, keepdims=True)) * inv
            stage[lane, at] = d.astype(jnp.bfloat16)

        store(lane).start()

    for w in range(WAVES):
        first_round(w)
        if w == 0:
            prepare()

        @pl.loop(1, HOPS - 1)
        def _(h):
            relay_round(w, h)
            if w == 0 and compute:
                pl.when(h == 2)(own_tile)
            if w > 0:
                @pl.when(h == 1)
                def _():
                    last_pieces(w - 1)

        last_round(w)
        group_pieces(w)

    for lane in (TEXT, IMAGE):
        @pl.loop(0, CHUNKS)
        def _(c):
            chunk = (WAVES - 1) * CHUNKS + c
            arrived(lane, LAST_SLOT, chunk)
            if compute:
                piece(lane, LAST_SLOT, pl.multiple_of(chunk * part, part), part)

        finish(lane)

    for lane in (TEXT, IMAGE):
        for h in range(HOPS):
            pltpu.make_async_remote_copy(
                src_ref=buf.at[lane, 0], dst_ref=buf.at[lane, 0], send_sem=send_sem.at[lane, h],
                recv_sem=recv_sem.at[lane, 0, 0], device_id=following, device_id_type=MESH,
            ).wait_send()
        store(lane).wait()

    def side_done(kind):
        pltpu.make_async_remote_copy(
            src_ref=buf.at[0, 0], dst_ref=buf.at[0, 0], send_sem=side_sem.at[kind],
            recv_sem=recv_sem.at[0, 0, 0], device_id=partner, device_id_type=MESH,
        ).wait_send()

    side_done(0)

    @pl.when(gives)
    def _():
        side_done(1)


COMPUTE = True


def shards(image_emb, text_emb, labels, log_scale, bias):
    rows, width = image_emb.shape
    block = (rows, width)
    whole = pl.BlockSpec(memory_space=pl.ANY)
    vmem = pl.BlockSpec(memory_space=pltpu.VMEM)
    smem = pl.BlockSpec(memory_space=pltpu.SMEM)
    macs = 11 * rows * rows * width
    return pl.pallas_call(
        functools.partial(kernel, rows, COMPUTE),
        name="relay",
        out_shape=[jax.ShapeDtypeStruct(block, jnp.bfloat16)] * 2,
        in_specs=[smem, smem, vmem, whole, whole],
        out_specs=[whole, whole],
        scratch_shapes=[
            pltpu.VMEM((2, *block), jnp.bfloat16),
            pltpu.VMEM((2, *block), jnp.bfloat16),
            pltpu.VMEM((2, *block), jnp.float32),
            pltpu.VMEM((rows // WAVES, width), jnp.bfloat16),
            pltpu.VMEM((2, *block), jnp.bfloat16),
            pltpu.VMEM((2, HOPS + 1, *block), jnp.bfloat16),
            pltpu.SemaphoreType.DMA((2,)),
            pltpu.SemaphoreType.DMA((2, HOPS)),
            pltpu.SemaphoreType.DMA((2, HOPS + 1, WAVES * CHUNKS)),
            pltpu.SemaphoreType.DMA((2,)),
            pltpu.SemaphoreType.DMA((2,)),
        ],
        compiler_params=pltpu.CompilerParams(
            collective_id=0, has_side_effects=True, vmem_limit_bytes=52 * 1024 * 1024
        ),
        cost_estimate=pl.CostEstimate(
            flops=2 * macs, bytes_accessed=8 * rows * width, transcendentals=5 * rows * rows
        ),
    )(log_scale, bias, labels.reshape(1, rows), image_emb, text_emb)


def solution(mesh):
    placed = (P(("group", "blk"), None), P(("group", "blk"), None), P(("group", "blk")), P(), P())
    return jax.shard_map(
        shards,
        mesh=mesh,
        in_specs=placed,
        out_specs=(P(("group", "blk"), None), P(("group", "blk"), None)),
        check_vma=False,
    )
```

time: 264 us -> 242 us (0.917)
  the two profiles are of different devices: /device:TPU:40 before, /device:TPU:1 now
where the time goes in v1:
time: 242 us
  Pallas kernels  237 us (98%)
  local copies, waits for them, and re-layouts  3.38 us (1%)
    pallas_call x1, Pallas kernels, shards(): pl.pallas_call(functools.partial(kernel, rows, COMPUTE), name='relay', ou...  237 us

profile of v1, /device:TPU:1, one launch (start us, length us, event | category | flops | bytes accessed | tf_op | source)
XLA Modules:
  0.0 241.9 jit_solution(862019326283453346)
XLA Ops:
  1.9 0.0 copy-start
  1.9 0.7 copy-done
  2.6 236.5 %relay.1 = (bf16[512,1152]{1,0:T(8,128)(2,1)S(1)}, bf16[512,1152]{1,0:T(8,128)(2,1)}) custom-call(f32[1]{0:T(128)S(6)} %copy.9.scale_ref, f32[1]{0:T(128)S(6)} %copy.10.bias_ref, s32[1,512]{1,0:T(1,128)S(1)} %bitcast.1, bf16[512,1152]{1,0:T(8,128)(2,1)} %image_ref.1, bf16[512,1152]{1,0:T(8,128)(2,1)} %text_ref.1), custom_call_target="tpu_custom_call" | custom-call | flops 6643777536 | bytes 4718592 | tf_op jit(solution)/shard_map/relay/pallas_call | solution.py:276
  239.1 0.0 copy-start.1
  239.2 1.0 copy.11
  240.2 0.7 copy-done.1
  240.8 1.0 copy.12
Async XLA Ops:
  1.9 0.7 copy-start
  239.1 1.7 copy-start.1

commit v2 on v1

--- a/solution.py
+++ b/solution.py
@@ -10,11 +10,15 @@
 EPS = 1e-06
 MESH = pl.DeviceIdType.MESH
 TEXT, IMAGE = 0, 1
-HOPS = 8
+LEGS = (1, 1, 1, 1, 1, 1, 1, 1)
 WAVES = 2
 CHUNKS = 4
-GROUP_SLOT, LAST_SLOT = 7, 8
+STORE = True
+HOPS = len(LEGS)
+GROUP_SLOT, LAST_SLOT = HOPS - 1, HOPS
 BAND = 128
+WIDE = 256
+UNIT = 128
 
 
 def dot_nt(a, b):
@@ -33,7 +37,7 @@
 
 def kernel(
     rows, compute, scale_ref, bias_ref, label_ref, image_ref, text_ref, gimage_ref, gtext_ref,
-    raw, unit, acc, piece_unit, stage, buf, load_sem, send_sem, recv_sem, side_sem, store_sem,
+    raw, unit, acc, piece_unit, last_unit, last_q, stage, buf, load_sem, send_sem, recv_sem, side_sem, store_sem,
 ):
     g, b = lax.axis_index("group"), lax.axis_index("blk")
     core, z_lo = lax.rem(g, 2), lax.div(g, 2)
@@ -53,7 +57,9 @@
         return jnp.where(lax.rem(z_at + 32, 8) == edge, 1 - c, c)
 
     step = way(core)
-    following, before = device(z + step, core, xy), device(z - step, core, xy)
+    middle = sorted(set(LEGS[1:-1]))
+    ahead = {leg: device(z + step * leg, core, xy) for leg in middle}
+    behind = [device(z - step * leg, core, xy) for leg in middle]
     partner = device(z, other, xy)
     first, first_from, last, last_from = [], [], [], []
     for lane in (TEXT, IMAGE):
@@ -79,9 +85,9 @@
         load.start()
 
     barrier = pltpu.get_barrier_semaphore()
-    for source in (before, partner, *first_from, *last_from):
+    for source in (*behind, partner, *first_from, *last_from):
         pl.semaphore_signal(barrier, inc=1, device_id=source, device_id_type=MESH)
-    pl.semaphore_wait(barrier, 6)
+    pl.semaphore_wait(barrier, 5 + len(behind))
 
     def chunk_rows(chunk):
         return pl.ds(pl.multiple_of(chunk * part, part), part)
@@ -94,9 +100,8 @@
         )
 
     def arrived(lane, slot, chunk):
-        hop(lane, buf.at[lane, slot], slot, 0, chunk, following).wait_recv()
-
-    own_side = core
+        hop(lane, buf.at[lane, slot], slot, 0, chunk, partner).wait_recv()
+
     lane_side = other
     gives = jnp.where(core == 0, z_lo != 7, z_lo != 0)
     takes_lane = jnp.where(core == 0, z_lo == 0, z_lo == 7)
@@ -108,38 +113,46 @@
             recv_sem=recv_sem.at[lane, GROUP_SLOT, chunk], device_id=partner, device_id_type=MESH,
         )
 
+    lanes = (other, core)
+
+    def pick(lane, pair):
+        return tuple(jnp.where(lane == TEXT, t, i) for t, i in zip(*pair))
+
     def first_round(w):
-        for lane in (TEXT, IMAGE):
-            @pl.loop(0, CHUNKS)
-            def _(c):
-                hop(lane, own[lane], 0, 0, w * CHUNKS + c, first[lane]).start()
-
-        for lane in (TEXT, IMAGE):
-            @pl.when(own_side == lane)
+        for way_core in (0, 1):
+            @pl.when(core == way_core)
             def _():
+                for lane in (1 - way_core, way_core):
+                    @pl.loop(0, CHUNKS)
+                    def _(c):
+                        hop(lane, own[lane], 0, 0, w * CHUNKS + c, first[lane]).start()
+
                 @pl.loop(0, CHUNKS)
                 def _(c):
-                    side(own[lane], lane, 0, w * CHUNKS + c).start()
+                    side(own[way_core], way_core, 0, w * CHUNKS + c).start()
 
     def relay_round(w, h):
-        for lane in (TEXT, IMAGE):
+        for lane in lanes:
             @pl.loop(0, CHUNKS)
             def _(c):
                 chunk = w * CHUNKS + c
                 arrived(lane, h - 1, chunk)
-                hop(lane, buf.at[lane, h - 1], h, h, chunk, following).start()
-
-                @pl.when((h == 1) & gives & (lane_side == lane))
-                def _():
-                    side(buf.at[lane, 0], lane, 1, chunk).start()
+                hop(lane, buf.at[lane, h - 1], h, h, chunk, ahead[LEGS[h]]).start()
+
+                if h == 1:
+                    @pl.when(gives & (lane_side == lane))
+                    def _():
+                        side(buf.at[lane, 0], lane, 1, chunk).start()
 
     def last_round(w):
-        for lane in (TEXT, IMAGE):
+        for lane in lanes:
+            to = pick(lane, last)
+
             @pl.loop(0, CHUNKS)
             def _(c):
                 chunk = w * CHUNKS + c
                 arrived(lane, HOPS - 2, chunk)
-                hop(lane, buf.at[lane, HOPS - 2], LAST_SLOT, HOPS - 1, chunk, last[lane]).start()
+                hop(lane, buf.at[lane, HOPS - 2], LAST_SLOT, HOPS - 1, chunk, to).start()
 
     scale = jnp.exp(jnp.full((1, 1), scale_ref[0], jnp.float32))
     shift_b = bias_ref[0]
@@ -166,38 +179,52 @@
             acc[IMAGE, at] = jnp.dot(q, unit[IMAGE], preferred_element_type=jnp.float32)
             acc[TEXT] += dot_tn(q, unit[TEXT, at])
 
-    def piece(lane, slot, start, count):
-        piece_unit[0:count] = unit_rows(buf[lane, slot, pl.ds(start, count)])[0].astype(jnp.bfloat16)
-
-        @pl.loop(0, rows // BAND)
+    def piece(lane, slot, start):
+        piece_unit[...] = unit_rows(buf[lane, slot, pl.ds(start, wave_rows)])[0].astype(jnp.bfloat16)
+
+        @pl.loop(0, rows // WIDE)
         def _(i):
-            at = pl.ds(pl.multiple_of(i * BAND, BAND), BAND)
-            s = scale * dot_nt(unit[1 - lane, at], piece_unit[0:count]) + shift_b
+            at = pl.ds(pl.multiple_of(i * WIDE, WIDE), WIDE)
+            s = scale * dot_nt(unit[1 - lane, at], piece_unit[...]) + shift_b
             q = jax.nn.sigmoid(s).astype(jnp.bfloat16)
-            acc[lane, at] += jnp.dot(q, piece_unit[0:count], preferred_element_type=jnp.float32)
+            acc[lane, at] += jnp.dot(q, piece_unit[...], preferred_element_type=jnp.float32)
 
     def group_pieces(w):
-        slot = jnp.where(takes_lane, HOPS - 2, GROUP_SLOT)
-        for lane in (TEXT, IMAGE):
-            from_lane = takes_lane & (core == lane)
-
-            @pl.when(jnp.logical_not(from_lane))
+        @pl.loop(0, 2)
+        def _(lane):
+            @pl.when(jnp.logical_not(takes_lane & (core == lane)))
             def _():
                 @pl.loop(0, CHUNKS)
                 def _(c):
                     arrived(lane, GROUP_SLOT, w * CHUNKS + c)
 
+                if compute:
+                    piece(lane, GROUP_SLOT, w * wave_rows)
+
+    def edge_piece(w):
+        @pl.when(takes_lane)
+        def _():
             if compute:
-                piece(lane, jnp.where(from_lane, HOPS - 2, GROUP_SLOT), w * wave_rows, wave_rows)
+                piece(core, HOPS - 2, w * wave_rows)
 
     def last_pieces(w):
-        for lane in (TEXT, IMAGE):
+        @pl.loop(0, 2)
+        def _(n):
+            lane = lax.rem(other + n, 2)
+
             @pl.loop(0, CHUNKS)
             def _(c):
                 arrived(lane, LAST_SLOT, w * CHUNKS + c)
 
             if compute:
-                piece(lane, LAST_SLOT, w * wave_rows, wave_rows)
+                piece(lane, LAST_SLOT, w * wave_rows)
+
+    def weigh(lane, n):
+        start = (WAVES - 1) * wave_rows + n * UNIT
+        u = unit_rows(buf[lane, LAST_SLOT, pl.ds(start, UNIT)])[0].astype(jnp.bfloat16)
+        last_unit[lane, pl.ds(n * UNIT, UNIT)] = u
+        s = scale * dot_nt(unit[1 - lane], u) + shift_b
+        last_q[lane, :, pl.ds(n * UNIT, UNIT)] = jax.nn.sigmoid(s).astype(jnp.bfloat16)
 
     def store(lane):
         out = (gimage_ref, gtext_ref)[lane]
@@ -208,47 +235,57 @@
         def _(i):
             at = pl.ds(pl.multiple_of(i * BAND, BAND), BAND)
             u, inv = unit_rows(raw[1 - lane, at])
-            d = scale * acc[lane, at]
+            last_part = jnp.dot(last_q[lane, at], last_unit[lane], preferred_element_type=jnp.float32)
+            d = scale * (acc[lane, at] + last_part)
             d = (d - u * jnp.sum(u * d, axis=-1, keepdims=True)) * inv
             stage[lane, at] = d.astype(jnp.bfloat16)
 
-        store(lane).start()
+        for which in (TEXT, IMAGE):
+            @pl.when(lane == which)
+            def _():
+                store(which).start()
 
     for w in range(WAVES):
         first_round(w)
         if w == 0:
             prepare()
 
-        @pl.loop(1, HOPS - 1)
-        def _(h):
+        for h in range(1, HOPS - 1):
             relay_round(w, h)
-            if w == 0 and compute:
-                pl.when(h == 2)(own_tile)
-            if w > 0:
-                @pl.when(h == 1)
-                def _():
+            if h == 1:
+                if w > 0:
                     last_pieces(w - 1)
+                elif compute:
+                    own_tile()
+            if h == 3:
+                group_pieces(w)
 
         last_round(w)
-        group_pieces(w)
-
-    for lane in (TEXT, IMAGE):
-        @pl.loop(0, CHUNKS)
-        def _(c):
-            chunk = (WAVES - 1) * CHUNKS + c
-            arrived(lane, LAST_SLOT, chunk)
+        edge_piece(w)
+
+    @pl.loop(0, 2)
+    def _(n):
+        lane = lax.rem(other + n, 2)
+
+        for n in range(wave_rows // UNIT):
+            @pl.loop(n * UNIT // part, (n + 1) * UNIT // part)
+            def _(c):
+                arrived(lane, LAST_SLOT, (WAVES - 1) * CHUNKS + c)
+
             if compute:
-                piece(lane, LAST_SLOT, pl.multiple_of(chunk * part, part), part)
-
-        finish(lane)
+                weigh(lane, n)
+
+        if STORE:
+            finish(lane)
 
     for lane in (TEXT, IMAGE):
         for h in range(HOPS):
             pltpu.make_async_remote_copy(
                 src_ref=buf.at[lane, 0], dst_ref=buf.at[lane, 0], send_sem=send_sem.at[lane, h],
-                recv_sem=recv_sem.at[lane, 0, 0], device_id=following, device_id_type=MESH,
+                recv_sem=recv_sem.at[lane, 0, 0], device_id=partner, device_id_type=MESH,
             ).wait_send()
-        store(lane).wait()
+        if STORE:
+            store(lane).wait()
 
     def side_done(kind):
         pltpu.make_async_remote_copy(
@@ -284,6 +321,8 @@
             pltpu.VMEM((2, *block), jnp.bfloat16),
             pltpu.VMEM((2, *block), jnp.float32),
             pltpu.VMEM((rows // WAVES, width), jnp.bfloat16),
+            pltpu.VMEM((2, rows // WAVES, width), jnp.bfloat16),
+            pltpu.VMEM((2, rows, rows // WAVES), jnp.bfloat16),
             pltpu.VMEM((2, *block), jnp.bfloat16),
             pltpu.VMEM((2, HOPS + 1, *block), jnp.bfloat16),
             pltpu.SemaphoreType.DMA((2,)),

time: 242 us -> 230 us (0.950)
  Pallas kernels: 237 us -> 223 us
    pallas_call x1, Pallas kernels: 237 us -> 223 us  [shards(): pl.pallas_call(functools.partial(kernel, rows, COMPUTE), name='relay', ou...]
where the time goes in v2:
time: 230 us; the launch traced here: 228 us
  Pallas kernels  223 us (97%)
  local copies, waits for them, and re-layouts  3.38 us (1%)
    pallas_call x1, Pallas kernels, shards(): pl.pallas_call(functools.partial(kernel, rows, COMPUTE), name='relay', ou...  223 us

profile of v2, /device:TPU:1, one launch (start us, length us, event | category | flops | bytes accessed | tf_op | source)
XLA Modules:
  0.0 227.9 jit_solution(9346465621957385502)
XLA Ops:
  1.9 0.0 copy-start
  1.9 0.7 copy-done
  2.6 222.5 %relay.1 = (bf16[512,1152]{1,0:T(8,128)(2,1)S(1)}, bf16[512,1152]{1,0:T(8,128)(2,1)}) custom-call(f32[1]{0:T(128)S(6)} %copy.9.scale_ref, f32[1]{0:T(128)S(6)} %copy.10.bias_ref, s32[1,512]{1,0:T(1,128)S(1)} %bitcast.1, bf16[512,1152]{1,0:T(8,128)(2,1)} %image_ref.1, bf16[512,1152]{1,0:T(8,128)(2,1)} %text_ref.1), custom_call_target="tpu_custom_call" | custom-call | flops 6643777536 | bytes 4718592 | tf_op jit(solution)/shard_map/relay/pallas_call | solution.py:313
  225.2 0.0 copy-start.1
  225.2 1.0 copy.11
  226.2 0.7 copy-done.1
  226.9 1.0 copy.12
Async XLA Ops:
  1.9 0.7 copy-start
  225.2 1.7 copy-start.1

commit v3 on v2

v3 whole, which is shorter than its diff:
```python
import functools

import jax
import jax.numpy as jnp
from jax import lax
from jax.experimental import pallas as pl
from jax.experimental.pallas import tpu as pltpu
from jax.sharding import PartitionSpec as P

EPS = 1e-06
MESH = pl.DeviceIdType.MESH
TEXT, IMAGE = 0, 1
HOPS = 8
TURNS = (3, 1)
WAVES = 2
CHUNKS = 4
GROUP_SLOT, LAST_SLOT, TURN_SLOT = HOPS - 1, HOPS, HOPS + 1
BAND = 128
WIDE = 256
UNIT = 128


def dot_nt(a, b):
    return lax.dot_general(a, b, (((1,), (1,)), ((), ())), preferred_element_type=jnp.float32)


def dot_tn(a, b):
    return lax.dot_general(a, b, (((0,), (0,)), ((), ())), preferred_element_type=jnp.float32)


def unit_rows(v):
    f = v.astype(jnp.float32)
    inv = lax.rsqrt(jnp.sum(f * f, axis=-1, keepdims=True) + EPS)
    return f * inv, inv


def kernel(
    rows, scale_hbm, bias_hbm, label_hbm, image_ref, text_ref, out_ref,
    scale_ref, bias_ref, label_ref, raw, unit, acc, inv_ref, piece_unit, last_unit, last_q, buf, load_sem, send_sem, recv_sem, side_sem, turn_sem,
):
    g, b = lax.axis_index("group"), lax.axis_index("blk")
    core, z_lo = lax.rem(g, 2), lax.div(g, 2)
    xy = lax.div(b, 2)
    z = lax.rem(b, 2) * 8 + z_lo
    other = 1 - core
    step = 2 * core - 1

    def device(z_to, core_to, xy_to):
        z_in = lax.rem(z_to + 32, 16)
        return lax.rem(z_in, 8) * 2 + core_to, lax.rem(xy_to + 16, 16) * 2 + lax.div(z_in, 8)

    def low(z_at):
        return lax.rem(z_at + 32, 8)

    def high(z_at):
        return lax.div(lax.rem(z_at + 32, 16), 8)

    def edge(kind):
        return jnp.where(kind == TEXT, 7, 0)

    def lane_core(kind, z_at, core_at):
        return jnp.where(low(z_at) == edge(kind), 1 - core_at, core_at)

    def swap(lane, z_at, value):
        ends = (low(z_at) == 0) | (low(z_at) == 7)
        return jnp.where((lane == 0) | ends, 1 - value, value)

    def turns(kind, z_source):
        return high(z_source) == jnp.where(kind == TEXT, 1, 0)

    def shift(kind):
        return jnp.where(kind == TEXT, 1, -1)

    partner = device(z, other, xy)
    ahead, behind = device(z + step, core, xy), device(z - step, core, xy)
    columns = (device(z, core, xy - 1), device(z, core, xy + 1))
    first, first_turn, last_from = [], [], []
    for kind in (TEXT, IMAGE):
        lane = lane_core(kind, z, core)
        first.append(device(z + 2 * lane - 1, lane, xy))
        first_turn.append(swap(lane, z, kind))
        last_from.append(device(z - (2 * lane - 1), lane, xy))
    leg = jnp.where(core == 0, *TURNS)
    first_from, turning, turn_to, last, last_kind = [], [], [], [], []
    for n in (0, 1):
        kind = swap(core, z - step, n)
        first_from.append(device(z - step, lane_core(kind, z - step, core), xy))
        kind = swap(core, z - step * leg, n)
        turning.append(turns(kind, z - step * leg))
        turn_to.append(device(z, core, xy + shift(kind)))
        kind = swap(core, z + step, n)
        last_kind.append(kind)
        last.append(device(z + step, lane_core(kind, z + step, core), xy))
    early = jnp.where(first_turn[TEXT] == 0, TEXT, IMAGE)

    own = (text_ref, image_ref)
    part = rows // (WAVES * CHUNKS)
    wave_rows = rows // WAVES

    loads = [pltpu.make_async_copy(own[l], raw.at[l], load_sem.at[l]) for l in (TEXT, IMAGE)]
    small = ((scale_hbm, scale_ref), (bias_hbm, bias_ref), (label_hbm, label_ref))
    loads += [pltpu.make_async_copy(src, dst, load_sem.at[2 + n]) for n, (src, dst) in enumerate(small)]
    for load in loads:
        load.start()

    barrier = pltpu.get_barrier_semaphore()
    for source in (partner, behind, *columns, *first_from, *last_from):
        pl.semaphore_signal(barrier, inc=1, device_id=source, device_id_type=MESH)
    pl.semaphore_wait(barrier, 8)

    def chunk_rows(chunk):
        return pl.ds(pl.multiple_of(chunk * part, part), part)

    def hop(src, at_n, slot, n, leg, chunk, to):
        at = chunk_rows(chunk)
        return pltpu.make_async_remote_copy(
            src_ref=src.at[at], dst_ref=buf.at[at_n, slot, at], send_sem=send_sem.at[n, leg],
            recv_sem=recv_sem.at[at_n, slot, chunk], device_id=to, device_id_type=MESH,
        )

    def send(src, at_n, slot, n, leg, w, c, to):
        hop(src, at_n, slot, n, leg, w * CHUNKS + c, to).start()

    def across(src, at_n, slot, way, chunk, to):
        at = chunk_rows(chunk)
        return pltpu.make_async_remote_copy(
            src_ref=src.at[at], dst_ref=buf.at[at_n, slot, at], send_sem=turn_sem.at[way],
            recv_sem=recv_sem.at[at_n, slot, chunk], device_id=to, device_id_type=MESH,
        )

    def arrived(n, slot, chunk):
        hop(buf.at[n, slot], n, slot, 0, 0, chunk, partner).wait_recv()

    side_kind = other
    side_turn = swap(core, z - step, side_kind)
    gives = jnp.where(core == 0, z_lo != 7, z_lo != 0)
    takes_lane = jnp.where(core == 0, z_lo == 0, z_lo == 7)
    returns = takes_lane & turns(core, z - 7 * step)
    return_to = device(z, core, xy - shift(core))

    def side(src, kind, way, chunk):
        at = chunk_rows(chunk)
        return pltpu.make_async_remote_copy(
            src_ref=src.at[at], dst_ref=buf.at[kind, GROUP_SLOT, at], send_sem=side_sem.at[way],
            recv_sem=recv_sem.at[kind, GROUP_SLOT, chunk], device_id=partner, device_id_type=MESH,
        )

    def first_round(w):
        for kinds in ((TEXT, IMAGE), (IMAGE, TEXT)):
            @pl.when(early == kinds[0])
            def _():
                for kind in kinds:
                    @pl.loop(0, CHUNKS)
                    def _(c):
                        n = first_turn[kind]
                        send(own[kind], n, 0, n, 0, w, c, first[kind])

        for kind in (TEXT, IMAGE):
            @pl.when(core == kind)
            def _():
                @pl.loop(0, CHUNKS)
                def _(c):
                    side(own[kind], kind, 0, w * CHUNKS + c).start()

    def relay_round(w, h):
        def relay(n, slot, to):
            @pl.loop(0, CHUNKS)
            def _(c):
                chunk = w * CHUNKS + c
                arrived(n, slot, chunk)
                send(buf.at[n, slot], n, h, n, h, w, c, to)

                if h == 1 and slot == 0:
                    @pl.when(gives & (side_turn == n))
                    def _():
                        side(buf.at[n, 0], side_kind, 1, chunk).start()

        if h not in TURNS:
            for n in (0, 1):
                relay(n, h - 1, ahead)
            return

        for n in (0, 1):
            turned = turning[n] & (leg == h)

            @pl.when(turned)
            def _():
                @pl.loop(0, CHUNKS)
                def _(c):
                    chunk = w * CHUNKS + c
                    arrived(n, h - 1, chunk)
                    across(buf.at[n, h - 1], n, TURN_SLOT, 0, chunk, turn_to[n]).start()

                    if h == 1:
                        @pl.when(gives & (side_turn == n))
                        def _():
                            side(buf.at[n, 0], side_kind, 1, chunk).start()

            @pl.when(jnp.logical_not(turned))
            def _():
                relay(n, h - 1, ahead)

        for n in (0, 1):
            @pl.when(turning[n] & (leg == h))
            def _():
                relay(n, TURN_SLOT, ahead)

    def last_round(w):
        for n in (0, 1):
            @pl.loop(0, CHUNKS)
            def _(c):
                chunk = w * CHUNKS + c
                arrived(n, HOPS - 2, chunk)
                send(buf.at[n, HOPS - 2], last_kind[n], LAST_SLOT, n, HOPS - 1, w, c, last[n])

                @pl.when(returns & (other == n))
                def _():
                    across(buf.at[n, HOPS - 2], core, GROUP_SLOT, 1, chunk, return_to).start()


    def prepare():
        for l in (TEXT, IMAGE):
            loads[l].wait()

            @pl.loop(0, rows // BAND)
            def _(i):
                at = pl.ds(pl.multiple_of(i * BAND, BAND), BAND)
                u, inv = unit_rows(raw[l, at])
                unit[l, at] = u.astype(jnp.bfloat16)
                inv_ref[l, at] = inv

    def own_tile():
        acc[TEXT] = jnp.zeros_like(acc[TEXT])

        @pl.loop(0, rows // BAND)
        def _(i):
            at = pl.ds(pl.multiple_of(i * BAND, BAND), BAND)
            s = scale * dot_nt(unit[TEXT, at], unit[IMAGE]) + shift_b
            text_row = lax.broadcasted_iota(jnp.int32, s.shape, 0) + i * BAND
            label = (text_row == label_ref[...]).astype(jnp.float32)
            q = (jax.nn.sigmoid(s) - label).astype(jnp.bfloat16)
            acc[IMAGE, at] = jnp.dot(q, unit[IMAGE], preferred_element_type=jnp.float32)
            acc[TEXT] += dot_tn(q, unit[TEXT, at])

    def piece(kind, n, slot, start):
        piece_unit[...] = unit_rows(buf[n, slot, pl.ds(start, wave_rows)])[0].astype(jnp.bfloat16)

        @pl.loop(0, rows // WIDE)
        def _(i):
            at = pl.ds(pl.multiple_of(i * WIDE, WIDE), WIDE)
            s = scale * dot_nt(unit[1 - kind, at], piece_unit[...]) + shift_b
            q = jax.nn.sigmoid(s).astype(jnp.bfloat16)
            acc[kind, at] += jnp.dot(q, piece_unit[...], preferred_element_type=jnp.float32)

    def group_pieces(w):
        @pl.loop(0, 2)
        def _(kind):
            @pl.when(jnp.logical_not(takes_lane & (core == kind)))
            def _():
                @pl.loop(0, CHUNKS)
                def _(c):
                    arrived(kind, GROUP_SLOT, w * CHUNKS + c)

                piece(kind, kind, GROUP_SLOT, w * wave_rows)

    def edge_piece(w):
        @pl.when(takes_lane)
        def _():
            @pl.when(returns)
            def _():
                @pl.loop(0, CHUNKS)
                def _(c):
                    arrived(core, GROUP_SLOT, w * CHUNKS + c)

            at_n, slot = jnp.where(returns, core, other), jnp.where(returns, GROUP_SLOT, HOPS - 2)
            piece(core, at_n, slot, w * wave_rows)

    def last_pieces(w):
        @pl.loop(0, 2)
        def _(n):
            kind = lax.rem(early + n, 2)

            @pl.loop(0, CHUNKS)
            def _(c):
                arrived(kind, LAST_SLOT, w * CHUNKS + c)

            piece(kind, kind, LAST_SLOT, w * wave_rows)

    def weigh(kind, n):
        start = (WAVES - 1) * wave_rows + n * UNIT
        u = unit_rows(buf[kind, LAST_SLOT, pl.ds(start, UNIT)])[0].astype(jnp.bfloat16)
        last_unit[kind, pl.ds(n * UNIT, UNIT)] = u
        s = scale * dot_nt(unit[1 - kind], u) + shift_b
        last_q[kind, :, pl.ds(n * UNIT, UNIT)] = jax.nn.sigmoid(s).astype(jnp.bfloat16)

    def finish(kind):
        @pl.loop(0, rows // BAND)
        def _(i):
            at = pl.ds(pl.multiple_of(i * BAND, BAND), BAND)
            inv = inv_ref[1 - kind, at]
            u = raw[1 - kind, at].astype(jnp.float32) * inv
            last_part = jnp.dot(last_q[kind, at], last_unit[kind], preferred_element_type=jnp.float32)
            d = scale * (acc[kind, at] + last_part)
            d = (d - u * jnp.sum(u * d, axis=-1, keepdims=True)) * inv
            out_ref[kind, at] = d.astype(jnp.bfloat16)

    waves = range(WAVES)
    for w in waves:
        first_round(w)
    for load in loads[2:]:
        load.wait()
    scale = jnp.exp(scale_ref[...])
    shift_b = bias_ref[...]
    prepare()
    for h in range(1, HOPS - 1):
        for w in waves:
            relay_round(w, h)
            if h == 3 + w:
                group_pieces(w)
        if h == 1:
            own_tile()
    for w in waves:
        last_round(w)
        edge_piece(w)
    for w in waves[:-1]:
        last_pieces(w)

    @pl.loop(0, 2)
    def _(n):
        kind = lax.rem(early + n, 2)

        for m in range(wave_rows // UNIT):
            @pl.loop(m * UNIT // part, (m + 1) * UNIT // part)
            def _(c):
                arrived(kind, LAST_SLOT, (WAVES - 1) * CHUNKS + c)

            weigh(kind, m)

        finish(kind)

    def done(sem):
        pltpu.make_async_remote_copy(
            src_ref=buf.at[0, 0], dst_ref=buf.at[0, 0], send_sem=sem,
            recv_sem=recv_sem.at[0, 0, 0], device_id=partner, device_id_type=MESH,
        ).wait_send()

    for n in (0, 1):
        for h in range(HOPS):
            done(send_sem.at[n, h])
    done(side_sem.at[0])
    done(turn_sem.at[0])

    @pl.when(gives)
    def _():
        done(side_sem.at[1])

    @pl.when(returns)
    def _():
        done(turn_sem.at[1])


def place(grads_ref, gimage_ref, gtext_ref, sem):
    copies = [
        pltpu.make_async_copy(grads_ref.at[n], out, sem.at[n]) for n, out in enumerate((gimage_ref, gtext_ref))
    ]
    for copy in copies:
        copy.start()
    for copy in copies:
        copy.wait()


def shards(image_emb, text_emb, labels, log_scale, bias):
    rows, width = image_emb.shape
    block = (rows, width)
    whole = pl.BlockSpec(memory_space=pl.ANY)
    vmem = pl.BlockSpec(memory_space=pltpu.VMEM)
    macs = 11 * rows * rows * width
    grads = pl.pallas_call(
        functools.partial(kernel, rows),
        name="relay",
        out_shape=pltpu.VMEM((2, *block), jnp.bfloat16),
        in_specs=[whole] * 5,
        out_specs=vmem,
        scratch_shapes=[
            pltpu.VMEM((1, 1), jnp.float32),
            pltpu.VMEM((1, 1), jnp.float32),
            pltpu.VMEM((1, rows), jnp.int32),
            pltpu.VMEM((2, *block), jnp.bfloat16),
            pltpu.VMEM((2, *block), jnp.bfloat16),
            pltpu.VMEM((2, *block), jnp.float32),
            pltpu.VMEM((2, rows, 1), jnp.float32),
            pltpu.VMEM((rows // WAVES, width), jnp.bfloat16),
            pltpu.VMEM((2, rows // WAVES, width), jnp.bfloat16),
            pltpu.VMEM((2, rows, rows // WAVES), jnp.bfloat16),
            pltpu.VMEM((2, HOPS + 2, *block), jnp.bfloat16),
            pltpu.SemaphoreType.DMA((5,)),
            pltpu.SemaphoreType.DMA((2, HOPS)),
            pltpu.SemaphoreType.DMA((2, HOPS + 2, WAVES * CHUNKS)),
            pltpu.SemaphoreType.DMA((2,)),
            pltpu.SemaphoreType.DMA((2,)),
        ],
        compiler_params=pltpu.CompilerParams(
            collective_id=0, has_side_effects=True, vmem_limit_bytes=52 * 1024 * 1024
        ),
        cost_estimate=pl.CostEstimate(
            flops=2 * macs, bytes_accessed=8 * rows * width, transcendentals=5 * rows * rows
        ),
    )(log_scale.reshape(1, 1), bias.reshape(1, 1), labels.reshape(1, rows), image_emb, text_emb)
    return pl.pallas_call(
        place,
        name="place",
        out_shape=[jax.ShapeDtypeStruct(block, jnp.bfloat16)] * 2,
        in_specs=[vmem],
        out_specs=[whole, whole],
        scratch_shapes=[pltpu.SemaphoreType.DMA((2,))],
        compiler_params=pltpu.CompilerParams(vmem_limit_bytes=1024 * 1024),
    )(grads)


def solution(mesh):
    placed = (P(("group", "blk"), None), P(("group", "blk"), None), P(("group", "blk")), P(), P())
    return jax.shard_map(
        shards,
        mesh=mesh,
        in_specs=placed,
        out_specs=(P(("group", "blk"), None), P(("group", "blk"), None)),
        check_vma=False,
    )
```

time: 230 us -> 227 us (0.987)
  local copies, waits for them, and re-layouts: 3.38 us -> 0 us
    unnamed x6 -> x0, local copies, waits for them, and re-layouts: 3.38 us -> none
    pallas_call x1 -> x2, Pallas kernels: 223 us -> 225 us  [the longest x1 223 us: shards(): pl.pallas_call(functools.partial(kernel, rows), name='relay', out_shape=p...]
where the time goes in v3:
time: 227 us
  Pallas kernels  225 us (99%)
    pallas_call x1, Pallas kernels, shards(): pl.pallas_call(functools.partial(kernel, rows), name='relay', out_shape=p...  223 us

profile of v3, /device:TPU:1, one launch (start us, length us, event | category | flops | bytes accessed | tf_op | source)
XLA Modules:
  0.0 226.7 jit_solution(5738364466472829408)
XLA Ops:
  1.9 223.4 %relay.1.grads_ref = bf16[2,512,1152]{2,1,0:T(8,128)(2,1)S(1)} custom-call(f32[1,1]{1,0:T(1,128)} %bitcast.3.scale_hbm, f32[1,1]{1,0:T(1,128)} %bitcast.4.bias_hbm, s32[1,512]{1,0:T(1,128)} %bitcast.5, bf16[512,1152]{1,0:T(8,128)(2,1)} %image_ref.1, bf16[512,1152]{1,0:T(8,128)(2,1)} %text_ref.1), custom_call_target="tpu_custom_call" | custom-call | flops 6643777536 | bytes 4718592 | tf_op jit(solution)/shard_map/relay/pallas_call | solution.py:378
  225.3 1.4 place.1

commit v4 on v3

--- a/solution.py
+++ b/solution.py
@@ -13,7 +13,7 @@
 HOPS = 8
 TURNS = (3, 1)
 WAVES = 2
-CHUNKS = 4
+CHUNKS = 2
 GROUP_SLOT, LAST_SLOT, TURN_SLOT = HOPS - 1, HOPS, HOPS + 1
 BAND = 128
 WIDE = 256
@@ -62,8 +62,7 @@
         return jnp.where(low(z_at) == edge(kind), 1 - core_at, core_at)
 
     def swap(lane, z_at, value):
-        ends = (low(z_at) == 0) | (low(z_at) == 7)
-        return jnp.where((lane == 0) | ends, 1 - value, value)
+        return jnp.where((lane == 0) | (low(z_at) == 7), 1 - value, value)
 
     def turns(kind, z_source):
         return high(z_source) == jnp.where(kind == TEXT, 1, 0)
@@ -91,7 +90,7 @@
         kind = swap(core, z + step, n)
         last_kind.append(kind)
         last.append(device(z + step, lane_core(kind, z + step, core), xy))
-    early = jnp.where(first_turn[TEXT] == 0, TEXT, IMAGE)
+    early = jnp.where((first_turn[TEXT] == 0) | ((core == 0) & (z == 0)), TEXT, IMAGE)
 
     own = (text_ref, image_ref)
     part = rows // (WAVES * CHUNKS)
@@ -135,6 +134,7 @@
     side_turn = swap(core, z - step, side_kind)
     gives = jnp.where(core == 0, z_lo != 7, z_lo != 0)
     takes_lane = jnp.where(core == 0, z_lo == 0, z_lo == 7)
+    taken_turn = swap(core, z - 7 * step, core)
     returns = takes_lane & turns(core, z - 7 * step)
     return_to = device(z, core, xy - shift(core))
 
@@ -153,7 +153,7 @@
                     @pl.loop(0, CHUNKS)
                     def _(c):
                         n = first_turn[kind]
-                        send(own[kind], n, 0, n, 0, w, c, first[kind])
+                        send(own[kind], n, 0, kind, 0, w, c, first[kind])
 
         for kind in (TEXT, IMAGE):
             @pl.when(core == kind)
@@ -213,7 +213,7 @@
                 arrived(n, HOPS - 2, chunk)
                 send(buf.at[n, HOPS - 2], last_kind[n], LAST_SLOT, n, HOPS - 1, w, c, last[n])
 
-                @pl.when(returns & (other == n))
+                @pl.when(returns & (taken_turn == n))
                 def _():
                     across(buf.at[n, HOPS - 2], core, GROUP_SLOT, 1, chunk, return_to).start()
 
@@ -272,7 +272,7 @@
                 def _(c):
                     arrived(core, GROUP_SLOT, w * CHUNKS + c)
 
-            at_n, slot = jnp.where(returns, core, other), jnp.where(returns, GROUP_SLOT, HOPS - 2)
+            at_n, slot = jnp.where(returns, core, taken_turn), jnp.where(returns, GROUP_SLOT, HOPS - 2)
             piece(core, at_n, slot, w * wave_rows)
 
     def last_pieces(w):

time: 227 us -> 223 us (0.982)
  Pallas kernels: 225 us -> 221 us
    pallas_call x1, Pallas kernels: 223 us -> 220 us  [shards(): pl.pallas_call(functools.partial(kernel, rows), name='relay', out_shape=p...]
where the time goes in v4:
time: 223 us
  Pallas kernels  221 us (99%)
    pallas_call x1, Pallas kernels, shards(): pl.pallas_call(functools.partial(kernel, rows), name='relay', out_shape=p...  220 us

profile of v4, /device:TPU:1, one launch (start us, length us, event | category | flops | bytes accessed | tf_op | source)
XLA Modules:
  0.0 223.0 jit_solution(11353676887694031470)
XLA Ops:
  1.9 219.6 %relay.1.grads_ref = bf16[2,512,1152]{2,1,0:T(8,128)(2,1)S(1)} custom-call(f32[1,1]{1,0:T(1,128)} %bitcast.3.scale_hbm, f32[1,1]{1,0:T(1,128)} %bitcast.4.bias_hbm, s32[1,512]{1,0:T(1,128)} %bitcast.5, bf16[512,1152]{1,0:T(8,128)(2,1)} %image_ref.1, bf16[512,1152]{1,0:T(8,128)(2,1)} %text_ref.1), custom_call_target="tpu_custom_call" | custom-call | flops 6643777536 | bytes 4718592 | tf_op jit(solution)/shard_map/relay/pallas_call | solution.py:378
  221.5 1.4 place.1

commit v5 on v4

--- a/solution.py
+++ b/solution.py
@@ -14,6 +14,7 @@
 TURNS = (3, 1)
 WAVES = 2
 CHUNKS = 2
+PARTS = 4
 GROUP_SLOT, LAST_SLOT, TURN_SLOT = HOPS - 1, HOPS, HOPS + 1
 BAND = 128
 WIDE = 256
@@ -360,9 +361,12 @@
 
 
 def place(grads_ref, gimage_ref, gtext_ref, sem):
-    copies = [
-        pltpu.make_async_copy(grads_ref.at[n], out, sem.at[n]) for n, out in enumerate((gimage_ref, gtext_ref))
-    ]
+    part = gimage_ref.shape[0] // PARTS
+    copies = []
+    for n, out in enumerate((gimage_ref, gtext_ref)):
+        for m in range(PARTS):
+            at = pl.ds(m * part, part)
+            copies.append(pltpu.make_async_copy(grads_ref.at[n, at], out.at[at], sem.at[n, m]))
     for copy in copies:
         copy.start()
     for copy in copies:
@@ -412,7 +416,7 @@
         out_shape=[jax.ShapeDtypeStruct(block, jnp.bfloat16)] * 2,
         in_specs=[vmem],
         out_specs=[whole, whole],
-        scratch_shapes=[pltpu.SemaphoreType.DMA((2,))],
+        scratch_shapes=[pltpu.SemaphoreType.DMA((2, PARTS))],
         compiler_params=pltpu.CompilerParams(vmem_limit_bytes=1024 * 1024),
     )(grads)
 

time: 223 us -> 223 us (level)
  no operation moved by 1% of the time
where the time goes in v5:
time: 223 us
  Pallas kernels  221 us (99%)
    pallas_call x1, Pallas kernels, shards(): pl.pallas_call(functools.partial(kernel, rows), name='relay', out_shape=p...  220 us

profile of v5, /device:TPU:1, one launch (start us, length us, event | category | flops | bytes accessed | tf_op | source)
XLA Modules:
  0.0 223.0 jit_solution(9974544496397166259)
XLA Ops:
  1.9 219.6 %relay.1.grads_ref = bf16[2,512,1152]{2,1,0:T(8,128)(2,1)S(1)} custom-call(f32[1,1]{1,0:T(1,128)} %bitcast.3.scale_hbm, f32[1,1]{1,0:T(1,128)} %bitcast.4.bias_hbm, s32[1,512]{1,0:T(1,128)} %bitcast.5, bf16[512,1152]{1,0:T(8,128)(2,1)} %image_ref.1, bf16[512,1152]{1,0:T(8,128)(2,1)} %text_ref.1), custom_call_target="tpu_custom_call" | custom-call | flops 6643777536 | bytes 4718592 | tf_op jit(solution)/shard_map/relay/pallas_call | solution.py:382
  221.5 1.5 place.1
